TPU v7x, 256 devices: a whole 4x4x8 slice. The times are simulated.
256 devices in a mesh: ctx: 8 (over z_hi, x), tp: 4 (over z_lo), dec: 8 (over y, core).
Axes of the slice: x: 4, y: 4, z: 8 (z_hi: 2, z_lo: 4; z = z_hi * 4 + z_lo), core: 2. Of those that a mesh axis runs over, the one named last changes fastest.
Arguments:
- stretch_query_rows: bfloat16 [2048, 8192], P('ctx', 'tp'), may hold values from -14 to 14
- stretch_key_rows: bfloat16 [2048, 1024], P('ctx', 'tp'), may hold values from -6 to 6
- stretch_value_rows: bfloat16 [2048, 1024], P('ctx', 'tp'), may hold values from -5 to 5
- prefix_key_rows: bfloat16 [32768, 1024], P(('ctx', 'dec'), 'tp'), may hold values from -12 to 12
- prefix_value_rows: bfloat16 [32768, 1024], P(('ctx', 'dec'), 'tp'), may hold values from -5 to 5
- offset: int32 [1], replicated, may hold values from 8192 to 32768
- decode_query_rows: bfloat16 [2, 128, 8, 1024], P(None, ('ctx', 'tp'), 'dec'), may hold values from -21 to 21
- decode_keys: bfloat16 [2, 128, 8, 128], P(None, ('ctx', 'tp'), 'dec'), may hold values from -13 to 13
- decode_value_rows: bfloat16 [2, 128, 8, 128], P(None, ('ctx', 'tp'), 'dec'), may hold values from -5 to 5
- cache_keys: bfloat16 [128, 8, 2048, 128], P(('ctx', 'tp'), 'dec'), may hold values from -12 to 12
- cached_value_rows: bfloat16 [128, 8, 2048, 128], P(('ctx', 'tp'), 'dec'), may hold values from -5 to 5
- cache_lengths: int32 [128], P(('ctx', 'tp')), may hold values from 2 to 2048, as said below
- head_slot_index: int32 [8], replicated, may hold values from 0 to 7, each once
Outputs:
- prefill_out: bfloat16 [2048, 8192], P(('ctx', 'dec'), 'tp')
- decode_output: bfloat16 [2, 128, 8, 1024], P(None, ('ctx', 'tp'), 'dec')
Inputs may be any that keep to these rules, and one draw needn't show every extreme that they name: `cache_lengths`: 2048 and 2 are each taken by some request in every draw. `head_slot_index`: each slot holds one head.
All inputs are finite; a program needn't handle non-finite values.
Results may differ from a plain program's by a relative error of at most 0.0012.
Values may be sent and summed in bfloat16 or wider, within the bound.
A program may use at most 256 MiB of HBM per device.

v0:
```python
import jax
import jax.numpy as jnp
from jax import lax
from jax.sharding import PartitionSpec as P

HEAD_SIZE = 128
QUERY_GROUP = 8


masked_score = -1e30


def online_update(running, scores, usable, values):
    best_so, denominator, numerator = running
    masked = jnp.where(usable[None, None], scores, masked_score)
    new_best = jnp.maximum(best_so, jnp.max(masked, axis=-1))
    weights = jnp.where(usable[None, None], jnp.exp(masked - new_best[..., None]), 0.0)
    factor = jnp.exp(best_so - new_best)
    denominator = denominator * factor + jnp.sum(weights, axis=-1)
    numerator = numerator * factor[..., None] + jnp.einsum(
        "hgrk,khd->hgrd", weights, values.astype(jnp.float32), precision=lax.Precision.HIGHEST
    )
    return (new_best, denominator, numerator)


def head_for(head_slot_index, slot_number):
    return jnp.sum(
        jnp.where(
            head_slot_index == slot_number, jnp.arange(head_slot_index.shape[0], dtype=jnp.int32), 0
        )
    )


def shards(
    stretch_query_rows,
    stretch_key_rows,
    stretch_value_rows,
    prefix_key_rows,
    prefix_value_rows,
    offset,
    decode_query_rows,
    decode_keys,
    decode_value_rows,
    cache_keys,
    cached_value_rows,
    cache_lengths,
    head_slot_index,
):
    ctx_count = lax.axis_size("ctx")
    tp_count = lax.axis_size("tp")
    dec_count = lax.axis_size("dec")
    ctx_id = lax.axis_index("ctx")
    tp_id = lax.axis_index("tp")
    dec_id = lax.axis_index("dec")
    scaling = HEAD_SIZE ** (-0.5)
    rows_here = stretch_query_rows.shape[0]
    heads_here = stretch_key_rows.shape[1] // HEAD_SIZE
    slots_here = cache_keys.shape[1]
    query_rows = stretch_query_rows.reshape(rows_here, heads_here, QUERY_GROUP, HEAD_SIZE)
    row_ids = ctx_id * rows_here + jnp.arange(rows_here, dtype=jnp.int32)
    prompt_end = offset[0]
    key_share = rows_here * ctx_count // dec_count
    key_begin = dec_id * key_share
    spread = (
        lax.all_gather(stretch_key_rows[None], ("ctx", "tp"), axis=0, tiled=True),
        lax.all_gather(stretch_value_rows[None], ("ctx", "tp"), axis=0, tiled=True),
    )

    def arrange(gathered):
        gathered = gathered.reshape(ctx_count, tp_count, rows_here, heads_here, HEAD_SIZE)
        return gathered.transpose(0, 2, 1, 3, 4).reshape(
            ctx_count * rows_here, tp_count * heads_here, HEAD_SIZE
        )

    every_key = arrange(spread[0])
    every_value = arrange(spread[1])
    mine_keys = lax.dynamic_slice_in_dim(every_key, tp_id * heads_here, heads_here, 1)
    mine_values = lax.dynamic_slice_in_dim(every_value, tp_id * heads_here, heads_here, 1)
    slot_key_rows = jnp.stack(
        [
            lax.dynamic_index_in_dim(
                every_key, head_for(head_slot_index, dec_id * slots_here + 0), 1, keepdims=False
            )
        ],
        axis=1,
    )
    slot_value_rows = jnp.stack(
        [
            lax.dynamic_index_in_dim(
                every_value, head_for(head_slot_index, dec_id * slots_here + 0), 1, keepdims=False
            )
        ],
        axis=1,
    )
    part_keys = lax.dynamic_slice_in_dim(mine_keys, key_begin, key_share, 0)
    part_values = lax.dynamic_slice_in_dim(mine_values, key_begin, key_share, 0)
    block_len = prefix_key_rows.shape[0]
    start_state = (
        jnp.full((heads_here, QUERY_GROUP, rows_here), masked_score, jnp.float32),
        jnp.zeros((heads_here, QUERY_GROUP, rows_here), jnp.float32),
        jnp.zeros((heads_here, QUERY_GROUP, rows_here, HEAD_SIZE), jnp.float32),
    )
    block_keys = lax.all_gather(prefix_key_rows, "ctx", axis=0, tiled=True).reshape(
        -1, heads_here, HEAD_SIZE
    )
    block_values = lax.all_gather(prefix_value_rows, "ctx", axis=0, tiled=True).reshape(
        -1, heads_here, HEAD_SIZE
    )
    key_count = block_keys.shape[0]
    whole_ids = jnp.arange(key_count, dtype=jnp.int32)
    source_dev = whole_ids // block_len
    positions = (source_dev * dec_count + dec_id) * block_len + whole_ids % block_len
    usable = jnp.broadcast_to(positions[None, :] < prompt_end, (rows_here, key_count))
    scores = (
        jnp.einsum("rhgd,khd->hgrk", query_rows, block_keys, preferred_element_type=jnp.float32)
        * scaling
    )
    running = online_update(start_state, scores, usable, block_values)
    key_ids = key_begin + jnp.arange(key_share, dtype=jnp.int32)
    usable = key_ids[None, :] <= row_ids[:, None]
    scores = (
        jnp.einsum("rhgd,khd->hgrk", query_rows, part_keys, preferred_element_type=jnp.float32)
        * scaling
    )
    best_so, denominator, numerator = online_update(running, scores, usable, part_values)
    rows_out = rows_here // dec_count
    row_top = lax.pmax(best_so, "dec")
    factor = jnp.exp(best_so - row_top)
    numer_part, denom_part = (
        lax.psum_scatter(numerator * factor[..., None], "dec", scatter_dimension=2, tiled=True),
        lax.psum_scatter(denominator * factor, "dec", scatter_dimension=2, tiled=True),
    )
    prefill_out = (
        (numer_part / denom_part[..., None])
        .transpose(2, 0, 1, 3)
        .reshape(rows_out, heads_here * QUERY_GROUP * HEAD_SIZE)
        .astype(jnp.bfloat16)
    )
    steps_here = decode_query_rows.shape[0]
    rows_dec = decode_query_rows.shape[1]
    dec_queries = decode_query_rows.reshape(
        steps_here, rows_dec, slots_here, QUERY_GROUP, HEAD_SIZE
    )
    cache_scores = (
        jnp.einsum("trsgd,rskd->trsgk", dec_queries, cache_keys, preferred_element_type=jnp.float32)
        * scaling
    )
    cache_ok = (jnp.arange(cache_keys.shape[2], dtype=jnp.int32)[None, :] < cache_lengths[:, None])[
        None, :, None, None, :
    ]
    stretch_scores = (
        jnp.einsum(
            "trsgd,ksd->trsgk", dec_queries, slot_key_rows, preferred_element_type=jnp.float32
        )
        * scaling
    )
    new_scores = (
        jnp.einsum(
            "trsgd,ursd->trsgu", dec_queries, decode_keys, preferred_element_type=jnp.float32
        )
        * scaling
    )
    step_ids = jnp.arange(steps_here, dtype=jnp.int32)
    new_ok = (step_ids[None, :] <= step_ids[:, None])[:, None, None, None, :]
    cache_scores = jnp.where(cache_ok, cache_scores, masked_score)
    new_scores = jnp.where(new_ok, new_scores, masked_score)
    row_top = jnp.maximum(
        jnp.maximum(jnp.max(cache_scores, axis=-1), jnp.max(stretch_scores, axis=-1)),
        jnp.max(new_scores, axis=-1),
    )[..., None]
    cache_weights = jnp.where(cache_ok, jnp.exp(cache_scores - row_top), 0.0)
    stretch_weights = jnp.exp(stretch_scores - row_top)
    new_weights = jnp.where(new_ok, jnp.exp(new_scores - row_top), 0.0)
    dec_denominator = (
        jnp.sum(cache_weights, axis=-1)
        + jnp.sum(stretch_weights, axis=-1)
        + jnp.sum(new_weights, axis=-1)
    )
    exact = lax.Precision.HIGHEST
    dec_numerator = jnp.einsum(
        "trsgk,rskd->trsgd", cache_weights, cached_value_rows.astype(jnp.float32), precision=exact
    )
    dec_numerator = dec_numerator + jnp.einsum(
        "trsgk,ksd->trsgd", stretch_weights, slot_value_rows.astype(jnp.float32), precision=exact
    )
    dec_numerator = dec_numerator + jnp.einsum(
        "trsgu,ursd->trsgd", new_weights, decode_value_rows.astype(jnp.float32), precision=exact
    )
    decode_output = (
        (dec_numerator / dec_denominator[..., None])
        .reshape(steps_here, rows_dec, slots_here, QUERY_GROUP * HEAD_SIZE)
        .astype(jnp.bfloat16)
    )
    return (prefill_out, decode_output)


def solution(mesh):
    placed = (
        P("ctx", "tp"),
        P("ctx", "tp"),
        P("ctx", "tp"),
        P(("ctx", "dec"), "tp"),
        P(("ctx", "dec"), "tp"),
        P(),
        P(None, ("ctx", "tp"), "dec", None),
        P(None, ("ctx", "tp"), "dec", None),
        P(None, ("ctx", "tp"), "dec", None),
        P(("ctx", "tp"), "dec", None, None),
        P(("ctx", "tp"), "dec", None, None),
        P(("ctx", "tp")),
        P(),
    )
    return jax.shard_map(
        shards,
        mesh=mesh,
        in_specs=placed,
        out_specs=(P(("ctx", "dec"), "tp"), P(None, ("ctx", "tp"), "dec", None)),
        check_vma=False,
    )
```

profile of v0, /device:TPU:1, one launch (start us, length us, event | category | flops | bytes accessed | tf_op | source)
XLA Modules:
  0.0 579.2 jit_solution(9771814423125160879)
XLA Ops:
  7.2 0.0 copy-start
  7.2 0.0 all-gather.7.cloned.1.call-start
  7.2 1.9 copy.54
  9.2 0.0 all-gather.7.cloned.1.call-update
  9.2 0.0 all-gather.11.cloned.1.call-start
  9.2 0.7 all-gather.11.cloned.1.call-update
  9.9 0.0 all-gather.13.cloned.1.call-start
  10.0 0.7 all-gather.13.cloned.1.call-update
  10.7 0.0 all-gather.9.cloned.1.call-start
  10.7 1.8 copy.57
  12.5 0.0 all-gather.9.cloned.1.call-update
  12.5 0.0 reduce-scatter.7.cloned.1.call-start
  13.3 1.5 copy.101
  14.7 0.1 broadcast_compare_fusion
  14.9 75.2 %all-gather.7.cloned.1.call-done = bf16[4096,256]{0,1:T(8,128)(2,1)} async-done(((bf16[512,256]{0,1:T(8,128)(2,1)}), bf16[4096,256]{0,1:T(8,128)(2,1)}) %all-gather.7.cloned.1.call-update) | async-done | bytes 2097168 | tf_op jit(solution)/shard_map/all_gather | solution.py:103
  90.0 28.0 %bitcast_reduce_fusion = (f32[2,8,256]{2,1,0:T(8,128)S(1)}, f32[2,4096,256,8]{2,1,3,0:T(8,128)}) fusion(pred[4096]{0:T(1024)(128)(4,1)S(1)} %fusion.66, bf16[4096,2,128,1]{0,2,3,1:T(8,128)(2,1)} %bitcast.178, bf16[256,2,8,128]{3,2,1,0:T(8,128)(2,1)S(1)} %bitcast.172), kind=kOutput, calls=%fused_computation.1 | convolution fusion | flops 4345294848 | bytes 70275072 | tf_op jit(solution)/shard_map/rhgd,khd->hgrk/dot_general | solution.py:115
  118.0 100.0 %all-gather.11.cloned.1.call-done = bf16[8192,256]{1,0:T(8,128)(2,1)} async-done(((bf16[256,256]{1,0:T(8,128)(2,1)}), bf16[8192,256]{1,0:T(8,128)(2,1)}) %all-gather.11.cloned.1.call-update) | async-done | bytes 4194320 | tf_op jit(solution)/shard_map/all_gather | solution.py:65
  218.0 6.9 %reshape.253 = bf16[8,4,256,2,128]{4,3,2,1,0:T(2,128)(2,1)} reshape(bf16[8192,256]{1,0:T(8,128)(2,1)} %all-gather.11.cloned.1.call-done) | data formatting | bytes 8388608 | tf_op jit(solution)/shard_map/reshape | solution.py:70
  224.9 5.2 copy.60
  230.1 139.4 %all-gather.13.cloned.1.call-done = bf16[8192,256]{1,0:T(8,128)(2,1)} async-done(((bf16[256,256]{1,0:T(8,128)(2,1)}), bf16[8192,256]{1,0:T(8,128)(2,1)}) %all-gather.13.cloned.1.call-update) | async-done | bytes 4194320 | tf_op jit(solution)/shard_map/all_gather | solution.py:66
  369.5 6.9 %reshape.255 = bf16[8,4,256,2,128]{4,3,2,1,0:T(2,128)(2,1)} reshape(bf16[8192,256]{1,0:T(8,128)(2,1)} %all-gather.13.cloned.1.call-done) | data formatting | bytes 8388608 | tf_op jit(solution)/shard_map/reshape | solution.py:70
  376.4 5.2 copy.62
  381.6 3.8 fusion.11
  385.4 42.8 %pmax.7 = f32[2,8,256]{2,1,0:T(8,128)S(1)} all-reduce(f32[2,8,256]{2,1,0:T(8,128)S(1)} %get-tuple-element.14), channel_id=1, replica_groups=mesh['ctx'=8,'tp'=4,'dec'=8] {'dec'}, use_global_device_ids=true, to_apply=%region_2.3 | all-reduce | flops 4096 | bytes 32768 | tf_op jit(solution)/shard_map/pmax | solution.py:127
  428.2 3.3 fusion.12
  431.6 21.5 %fusion.2 = f32[2,8,256]{2,1,0:T(8,128)S(1)} fusion(f32[2,4096,256,8]{2,1,3,0:T(8,128)} %get-tuple-element.19, f32[2,8,256]{2,1,0:T(8,128)S(1)} %get-tuple-element.15, pred[4096]{0:T(1024)(128)(4,1)S(1)} %fusion.66), kind=kLoop, calls=%fused_computation.5 | loop fusion | flops 83881984 | bytes 67145728 | tf_op jit(solution)/shard_map/reduce_sum | solution.py:19
  453.1 0.2 copy.99
  453.3 0.8 reshape.281
  454.1 7.3 %fusion.13 = f32[2,8,256,128]{3,2,1,0:T(8,128)} fusion(f32[2,256,256,8]{2,1,3,0:T(8,128)} %get-tuple-element.21, f32[2,8,256]{2,1,0:T(8,128)S(1)} %get-tuple-element.14, pred[256,256]{0,1:T(8,128)(4,1)S(1)} %broadcast_compare_fusion, bf16[2048,8,128]{2,0,1:T(8,128)(2,1)} %bitcast.176, s32[]{:T(128)S(6)} %select_n.82, s32[]{:T(128)S(6)} %select_n.84), kind=kOutput, calls=%fused_computation.17 | convolution fusion | flops 1614807040 | bytes 6504456 | tf_op jit(solution)/shard_map/hgrk,khd->hgrd/dot_general | solution.py:20
  461.4 0.0 reduce-scatter.7.cloned.1.call-update
  461.5 0.3 reduce-scatter.5.cloned.1.call-start
  461.7 6.4 %all-gather.9.cloned.1.call-done = bf16[4096,256]{0,1:T(8,128)(2,1)} async-done(((bf16[512,256]{0,1:T(8,128)(2,1)}), bf16[4096,256]{0,1:T(8,128)(2,1)}) %all-gather.9.cloned.1.call-update) | async-done | bytes 2097168 | tf_op jit(solution)/shard_map/all_gather | solution.py:106
  468.1 0.0 copy-start.6
  468.1 0.0 copy-start.2
  468.1 0.0 copy-start.5
  468.1 0.0 copy-start.4
  468.1 71.7 %add_multiply_fusion = f32[2,8,256,128]{3,2,1,0:T(8,128)} fusion(f32[2,8,256,128]{3,2,1,0:T(8,128)} %fusion.13, bf16[4096,2,128,1]{0,2,3,1:T(8,128)(2,1)} %bitcast.196, f32[2,4096,256,8]{2,1,3,0:T(8,128)} %get-tuple-element.19, f32[2,8,256]{2,1,0:T(8,128)S(1)} %get-tuple-element.15, pred[4096]{0:T(1024)(128)(4,1)S(1)} %fusion.66, ...), kind=kOutput, calls=%fused_computation.27 | convolution fusion | flops 25839009792 | bytes 73469952 | tf_op jit(solution)/shard_map/hgrk,khd->hgrd/dot_general | solution.py:20
  539.8 0.0 reduce-scatter.5.cloned.1.call-update
  539.8 0.0 copy-done.6
  539.8 0.6 fusion.79
  541.7 0.0 copy-done.2
  542.4 0.0 copy-start.1
  542.5 0.0 copy-done.5
  542.5 0.2 convolution_multiply_fusion.2
  542.6 0.1 fusion.72
  542.7 0.0 copy-done.4
  542.7 0.1 iota_compare_fusion
  542.8 0.0 copy-done
  542.8 0.7 fusion.90
  543.6 1.4 fusion.91
  545.0 0.1 fusion.87
  545.1 0.0 copy-done.3
  545.1 0.2 convolution_bitcast_fusion
  545.3 0.3 fusion.45
  545.7 0.0 copy-done.1
  545.7 1.1 fusion.31
  546.7 1.5 fusion.34
  548.3 0.6 copy.75
  548.9 0.8 reshape.282
  549.7 0.1 copy.100
  549.8 20.8 %reduce-scatter.5.cloned.1.call-done = f32[2,8,32,128]{3,2,1,0:T(8,128)} async-done(((f32[2,8,256,128]{3,2,1,0:T(8,128)}), f32[2,8,32,128]{3,2,1,0:T(8,128)}) %reduce-scatter.5.cloned.1.call-update) | async-done | bytes 262160 | tf_op jit(solution)/shard_map/reduce_scatter | solution.py:130
  570.5 1.1 fusion.55
  571.6 0.1 copy.64
  571.7 0.7 copy.137
  (11 shorter events, 0.1 us)
Async XLA Ops:
  7.2 535.7 %copy-start = (bf16[4,1,2048,128]{3,2,1,0:T(8,128)(2,1)S(1)}, bf16[4,1,2048,128]{3,2,1,0:T(8,128)(2,1)}, u32[]{:S(2)}) copy-start(bf16[4,1,2048,128]{3,2,1,0:T(8,128)(2,1)} %param.22) | copy-start | bytes 6291460
  7.2 82.8 %all-gather.7.cloned.1.call-start = ((), (), s32[]{:S(2)}) async-start(), calls=%async_computation.2 | async-start | bytes 2359296 | tf_op jit(solution)/shard_map/all_gather | solution.py:103
  9.2 208.8 %all-gather.11.cloned.1.call-start = ((), (), s32[]{:S(2)}) async-start(), calls=%async_computation.5 | async-start | bytes 4325376 | tf_op jit(solution)/shard_map/all_gather | solution.py:65
  9.9 359.6 %all-gather.13.cloned.1.call-start = ((), (), s32[]{:S(2)}) async-start(), calls=%async_computation.6 | async-start | bytes 4325376 | tf_op jit(solution)/shard_map/all_gather | solution.py:66
  10.7 457.4 %all-gather.9.cloned.1.call-start = ((), (), s32[]{:S(2)}) async-start(), calls=%async_computation.3 | async-start | bytes 2359296 | tf_op jit(solution)/shard_map/all_gather | solution.py:106
  12.5 536.4 %reduce-scatter.7.cloned.1.call-start = ((), (), s32[]{:S(2)}) async-start(), calls=%async_computation.7 | async-start | bytes 147456
  461.5 109.1 %reduce-scatter.5.cloned.1.call-start = ((), (), s32[]{:S(2)}) async-start(), calls=%async_computation.4 | async-start | bytes 2359296 | tf_op jit(solution)/shard_map/reduce_scatter | solution.py:130
  468.1 71.7 %copy-start.6 = (s32[8]{0:T(128)S(1)}, s32[8]{0:T(128)}, u32[]{:S(2)}) copy-start(s32[8]{0:T(128)} %param.25) | copy-start | bytes 100
  468.1 73.6 %copy-start.2 = (bf16[2,4,1,1024]{3,1,2,0:T(4,128)(2,1)S(1)}, bf16[2,4,1,1024]{3,1,2,0:T(4,128)(2,1)}, u32[]{:S(2)}) copy-start(bf16[2,4,1,1024]{3,1,2,0:T(4,128)(2,1)} %param.19) | copy-start | bytes 49156
  468.1 74.3 %copy-start.5 = (bf16[2,4,1,128]{3,1,2,0:T(4,128)(2,1)S(1)}, bf16[2,4,1,128]{3,1,2,0:T(4,128)(2,1)}, u32[]{:S(2)}) copy-start(bf16[2,4,1,128]{3,1,2,0:T(4,128)(2,1)} %param.20) | copy-start | bytes 6148
  468.1 74.6 %copy-start.4 = (s32[4]{0:T(128)S(1)}, s32[4]{0:T(128)}, u32[]{:S(2)}) copy-start(s32[4]{0:T(128)} %param.24) | copy-start | bytes 52
  539.8 5.3 copy-start.3
  542.4 3.3 copy-start.1
Sparse Core Ops, SparseCore 0:
  10.5 79.4 all-gather.6
  91.8 126.1 all-gather.10
  219.8 149.6 all-gather.12
  371.8 96.2 all-gather.8
  471.0 27.6 reduce-scatter.6
  539.9 30.5 reduce-scatter.4
where the time goes:
time: 582 us; the launch traced here: 579 us
  waiting for transfers between devices  343 us (59%)
  matrix products  116 us (20%)
  blocking collectives  42.8 us (7%)
  local copies, waits for them, and re-layouts  32.7 us (6%)
  other arithmetic  27.3 us (5%)
  between operations  16.9 us (3%)
    all_gather x1, waiting for transfers between devices, shards(): lax.all_gather(stretch_value_rows[None], ('ctx', 'tp'), axis=0, tiled=True)  139 us
    all_gather x1, waiting for transfers between devices, shards(): lax.all_gather(stretch_key_rows[None], ('ctx', 'tp'), axis=0, tiled=True)  100 us
    dot_general x2, matrix products, online_update(): jnp.einsum('hgrk,khd->hgrd', weights, values.astype(jnp.float32), precisi...  79 us
    all_gather x1, waiting for transfers between devices, shards(): lax.all_gather(prefix_key_rows, 'ctx', axis=0, tiled=True)  75.2 us
    pmax x1, blocking collectives, shards(): row_top = lax.pmax(best_so, 'dec')  42.8 us
    dot_general x1, matrix products, shards(): jnp.einsum('rhgd,khd->hgrk', query_rows, block_keys, preferred_element_ty...  28 us
    reduce_sum x2, other arithmetic, online_update(): denominator = denominator * factor + jnp.sum(weights, axis=-1)  24.8 us
    reshape x4, local copies, waits for them, and re-layouts, arrange(): gathered.reshape(ctx_count, tp_count, rows_here, heads_here, HEAD_SIZE)  24.2 us
  transfers between devices with their start and end apart: 6, of which 5 were waited for; matrix products, arithmetic and copies ran while one was open for 30% of the time, Pallas kernels for 0%

commit v1 on v0

v1 whole, which is shorter than its diff:
```python
import functools

import jax
import jax.numpy as jnp
from jax import lax
from jax.experimental import pallas as pl
from jax.experimental.pallas import tpu as pltpu
from jax.sharding import PartitionSpec as P

HEAD = 128
GROUP = 8
BLOCK = 512
ROWS = 256
CACHE = 2048
NEG = -1e30
SCALE = HEAD**-0.5 * 1.4426950408889634
BF = jnp.bfloat16
F32 = jnp.float32
NT = (((1,), (1,)), ((), ()))
MESH = pl.DeviceIdType.MESH

OWN, L, R, O, Z, ZL, ZR, ZO = range(8)
ORDER = [
    (0, OWN),
    (1, OWN),
    (0, L),
    (0, R),
    (0, O),
    (1, L),
    (1, R),
    (0, Z),
    (0, ZL),
    (0, ZR),
    (1, O),
    (0, ZO),
    (1, Z),
    (1, ZL),
    (1, ZR),
    (1, ZO),
]


def nt_dot(a, b):
    return lax.dot_general(a, b, NT, preferred_element_type=F32)


def dot(a, b):
    return jnp.dot(a, b, preferred_element_type=F32)


def split(p):
    hi = p.astype(BF)
    return hi, (p - hi.astype(F32)).astype(BF)


def kernel(
    blocks,
    offset_ref,
    slot_index_ref,
    lengths_ref,
    q_ref,
    pk_ref,
    pv_ref,
    sk_ref,
    sv_ref,
    dq_ref,
    dk_ref,
    dv_ref,
    ck_hbm,
    cv_hbm,
    out_ref,
    dec_ref,
    ck,
    cv,
    qx,
    kbuf,
    vbuf,
    small,
    cand,
    scat,
    dqall,
    kst,
    vst,
    vslot,
    dres,
    dret,
    dec_o,
    dec_l,
    s_a,
    s_b,
    x_a,
    x_b,
    m_ref,
    l_ref,
    acc_ref,
    obuf,
    cbuf,
    ybuf,
    cache_sem,
    send_sem,
    recv_sem,
    small_send,
    small_recv,
    scat_send,
    scat_recv,
    dq_send,
    dq_recv,
    dret_send,
    dret_recv,
    core_send,
    core_recv,
    y_send,
    y_recv,
):
    c = lax.axis_index("ctx")
    t = lax.axis_index("tp")
    d = lax.axis_index("dec")
    zh, x = c // 4, c % 4
    y, co = d // 2, d % 2

    def ctx_at(dz, dx):
        return ((zh + dz) % 2) * 4 + (x + dx) % 4

    slots = {
        OWN: ctx_at(0, 0),
        L: ctx_at(0, 3),
        R: ctx_at(0, 1),
        O: ctx_at(0, 2),
        Z: ctx_at(1, 0),
        ZL: ctx_at(1, 3),
        ZR: ctx_at(1, 1),
        ZO: ctx_at(1, 2),
    }
    dev = {k: (slots[k], t, d) for k in (L, R, O, Z)}
    tp_peer = [(c, (t + i) % 4, d) for i in (1, 2, 3)]
    core_peer = (c, t, y * 2 + 1 - co)
    y_peer = [(c, t, ((y + i) % 4) * 2 + co) for i in (1, 2, 3)]

    def remote(src, dst, ss, rs, to):
        return pltpu.make_async_remote_copy(
            src_ref=src, dst_ref=dst, send_sem=ss, recv_sem=rs, device_id=to, device_id_type=MESH
        )

    def when(cond, f):
        if cond is True:
            f()
        else:
            pl.when(cond)(f)

    def exists(which):
        return True if blocks >= 8 else slots[which] < blocks

    cache_copies = []
    for r in range(4):
        for i, (hbm, vmem) in enumerate(((ck_hbm, ck), (cv_hbm, cv))):
            cp = pltpu.make_async_copy(hbm.at[r], vmem.at[r], cache_sem.at[r, i])
            cp.start()
            cache_copies.append(cp)

    row_id = lax.broadcasted_iota(jnp.int32, (BLOCK, HEAD), 0)
    lane_id = lax.broadcasted_iota(jnp.int32, (BLOCK, HEAD), 1)

    def fill(i, carry):
        limit = offset_ref[0] - (i * 8 + d) * BLOCK
        bias = jnp.where((lane_id == 0) & (row_id >= limit), NEG, 0.0).astype(BF)
        kbuf[0, i, :, HEAD:] = bias
        kbuf[1, i, :, HEAD:] = bias
        return carry

    lax.fori_loop(0, blocks, fill, 0)

    barrier = pltpu.get_barrier_semaphore()
    peers = [dev[L], dev[R], dev[O], dev[Z], *tp_peer, core_peer, *y_peer]
    for p in peers:
        pl.semaphore_signal(barrier, inc=1, device_id=p, device_id_type=MESH)

    me = slots[OWN]
    for h in range(2):
        kbuf[h, me, :, :HEAD] = pk_ref[:, h * HEAD : (h + 1) * HEAD]
        vbuf[h, me] = pv_ref[:, h * HEAD : (h + 1) * HEAD].T

    my_head = 0
    for h in range(8):
        my_head = my_head + jnp.where(slot_index_ref[h] == d, h, 0)
    odd = my_head % 2 == 1
    for i, ref in enumerate((sk_ref, sv_ref)):
        chosen = jnp.where(odd, ref[:, HEAD:], ref[:, :HEAD])
        for q in range(4):
            cand[q, i] = chosen[q * 64 : (q + 1) * 64]
        mine = pl.ds(pl.multiple_of(d * 32, 32), 32)
        for h in range(2):
            small[me, (2 * i + h) * 32 : (2 * i + h + 1) * 32, :] = ref[mine, h * HEAD : (h + 1) * HEAD]
    scat[t] = cand[t]
    dqall[t] = dq_ref[...]

    pl.semaphore_wait(barrier, len(peers))

    def copy_k(h, which, to, n):
        s = slots[which]
        ref = kbuf.at[h, s, :, pl.ds(0, HEAD)]
        return remote(ref, ref, send_sem.at[h, n], recv_sem.at[h, s, 0], dev[to])

    def copy_v(h, which, to, n):
        s = slots[which]
        ref = vbuf.at[h, s]
        return remote(ref, ref, send_sem.at[h, n], recv_sem.at[h, s, 1], dev[to])

    own_sends = [(OWN, 0, Z, 0), (OWN, 0, L, 1), (OWN, 0, R, 2), (OWN, 1, Z, 3), (OWN, 1, L, 4), (OWN, 1, R, 5)]
    z_sends = [(Z, 0, L, 6), (Z, 0, R, 7), (Z, 1, L, 8), (Z, 1, R, 9)]
    forwards = {
        L: [(L, 0, R, 10)],
        R: [(R, 1, L, 11)],
        ZL: [(ZL, 0, R, 12)],
        ZR: [(ZR, 1, L, 13)],
        Z: z_sends,
    }

    def make(h, s):
        return (copy_v if s[1] else copy_k)(h, s[0], s[2], s[3])

    def start_all(h, sends):
        for s in sends:
            make(h, s).start()

    def arrive(h, which):
        def go():
            copy_k(h, which, L, 0).wait_recv()
            copy_v(h, which, L, 0).wait_recv()
            start_all(h, forwards.get(which, []))

        when(exists(which), go)

    for h in range(2):
        when(exists(OWN), functools.partial(start_all, h, own_sends))
        if h == 0:
            scat_copies = []
            dq_copies = []
            for i in range(3):
                q = (t + 1 + i) % 4
                cp = remote(cand.at[q], scat.at[t], scat_send.at[i], scat_recv.at[t], tp_peer[i])
                cp.start()
                scat_copies.append(cp)
                cp = remote(dqall.at[t], dqall.at[t], dq_send.at[i], dq_recv.at[t], tp_peer[i])
                cp.start()
                dq_copies.append(cp)

    one_lane = (lax.broadcasted_iota(jnp.int32, (ROWS, HEAD), 1) == 0).astype(F32).astype(BF)
    for j in range(16):
        qx[j, :, :HEAD] = q_ref[:, j * HEAD : (j + 1) * HEAD]
        qx[j, :, HEAD:] = one_lane
    m_ref[...] = jnp.full(m_ref.shape, NEG, F32)
    l_ref[...] = jnp.zeros(l_ref.shape, F32)
    acc_ref[...] = jnp.zeros(acc_ref.shape, F32)

    def score(h, slot, g, s_ref, x_ref):
        keys = kbuf[h, slot]
        for u in range(2):
            s = nt_dot(keys, qx[h * 8 + g * 2 + u])
            s_ref[u] = s
            x_ref[u] = jnp.max(s, axis=0, keepdims=True) * SCALE

    def update(j, s, top, vt):
        before = m_ref[j]
        now = jnp.maximum(before, top)
        p = jnp.exp2(s * SCALE - now)
        fade = jnp.exp2(before - now)
        l_ref[j] = l_ref[j] * fade + jnp.sum(p, axis=0, keepdims=True)
        m_ref[j] = now
        hi, lo = split(p)
        acc_ref[j] = acc_ref[j] * fade + (dot(vt, hi) + dot(vt, lo))

    def absorb(h, slot, g, s_ref, x_ref):
        for u in range(2):
            update(h * 8 + g * 2 + u, s_ref[u], x_ref[u], vbuf[h, slot])

    def flash_block(h, slot):
        score(h, slot, 0, s_a, x_a)

        def body(i, carry):
            g = 2 * i
            score(h, slot, g + 1, s_b, x_b)
            absorb(h, slot, g, s_a, x_a)
            score(h, slot, jnp.minimum(g + 2, 3), s_a, x_a)
            absorb(h, slot, g + 1, s_b, x_b)
            return carry

        lax.fori_loop(0, 2, body, 0)

    def small_copy(which, to, n):
        ref = small.at[slots[which]]
        return remote(ref, ref, small_send.at[n], small_recv.at[slots[which]], dev[to])

    def pick_slot_share():
        for cp in dq_copies + scat_copies:
            cp.wait_send()
        for i in range(3):
            src = (t + 3 - i) % 4
            remote(cand.at[0], scat.at[src], scat_send.at[i], scat_recv.at[src], tp_peer[i]).wait_recv()
        source = my_head // 2
        for i in range(2):
            share = scat[0, i]
            for q in range(1, 4):
                share = jnp.where(source == q, scat[q, i], share)
            small[me, 128 + 64 * i : 192 + 64 * i, :] = share
        for n, to in enumerate((Z, L, R, O)):
            small_copy(OWN, to, n).start()

    def pass_small():
        small_copy(Z, L, 0).wait_recv()
        for n, to in enumerate((L, R, O)):
            small_copy(Z, to, 4 + n).start()

    def take_small():
        for which in (L, R, O, ZL, ZR, ZO):
            small_copy(which, L, 0).wait_recv()
        for h in range(2):
            kst[h] = small[:, h * 32 : (h + 1) * 32, :].reshape(ROWS, HEAD)
            vst[h] = small[:, 64 + h * 32 : 96 + h * 32, :].reshape(ROWS, HEAD).T
        vslot[...] = small[:, 192:256, :].reshape(BLOCK, HEAD).T

    def stretch_part():
        kk = lax.broadcasted_iota(jnp.int32, (ROWS, ROWS), 0)
        key_row = (kk // 32) * ROWS + d * 32 + kk % 32
        query_row = c * ROWS + lax.broadcasted_iota(jnp.int32, (ROWS, ROWS), 1)
        usable = key_row <= query_row

        def body(i, carry):
            h = i // 4
            for u in range(2):
                j = 2 * i + u
                s = jnp.where(usable, nt_dot(kst[h], qx[j, :, :HEAD]), NEG)
                update(j, s, jnp.max(s, axis=0, keepdims=True) * SCALE, vst[h])
            return carry

        lax.fori_loop(0, 8, body, 0)

    def decode_cache():
        for cp in cache_copies:
            cp.wait()
        step_row = lax.broadcasted_iota(jnp.int32, (16, 1), 0) >= 8
        for r in range(4):
            q = dq_ref[r * 16 : (r + 1) * 16, :]
            qf = q.astype(F32)
            s = nt_dot(q, ck[r]) * SCALE
            s = jnp.where(lax.broadcasted_iota(jnp.int32, (16, CACHE), 1) < lengths_ref[r], s, NEG)
            new = []
            for u in range(2):
                sn = jnp.sum(qf * dk_ref[u * 4 + r : u * 4 + r + 1, :].astype(F32), axis=1, keepdims=True) * SCALE
                new.append(jnp.where(step_row, sn, NEG) if u else sn)
            top = jnp.maximum(jnp.max(s, axis=1, keepdims=True), jnp.maximum(new[0], new[1]))
            p = jnp.exp2(s - top)
            pn = [jnp.exp2(sn - top) for sn in new]
            total = jnp.sum(p, axis=1, keepdims=True) + pn[0] + pn[1]
            hi, lo = split(p)
            mixed = dot(jnp.concatenate([hi, lo], axis=0), cv[r])
            mixed = mixed[:16] + mixed[16:]
            for u in range(2):
                mixed = mixed + pn[u] * dv_ref[u * 4 + r : u * 4 + r + 1, :].astype(F32)
            dec_o[r * 16 : (r + 1) * 16, :] = mixed / total
            dec_l[r * 16 : (r + 1) * 16, :] = jnp.broadcast_to(top + jnp.log2(total), (16, HEAD))

    dret_copies = [
        remote(dres.at[(t + 1 + i) % 4], dret.at[t], dret_send.at[i], dret_recv.at[t], tp_peer[i]) for i in range(3)
    ]

    def decode_stretch():
        for i in range(3):
            src = (t + 3 - i) % 4
            remote(dqall.at[src], dqall.at[src], dq_send.at[i], dq_recv.at[src], tp_peer[i]).wait_recv()
        keys = small[:, 128:192, :].reshape(BLOCK, HEAD)
        s = nt_dot(keys, dqall[...].reshape(4 * 64, HEAD)) * SCALE
        top = jnp.max(s, axis=0, keepdims=True)
        p = jnp.exp2(s - top)
        total = jnp.sum(p, axis=0, keepdims=True)
        hi, lo = split(p)
        o = ((dot(vslot[...], hi) + dot(vslot[...], lo)) / total).T
        lse = jnp.broadcast_to(top + jnp.log2(total), (HEAD, 256)).T
        for q in range(4):
            dres[q, 0] = o[q * 64 : (q + 1) * 64]
            dres[q, 1] = lse[q * 64 : (q + 1) * 64]
        dret[t] = dres[t]
        for cp in dret_copies:
            cp.start()

    def decode_finish():
        for i in range(3):
            src = (t + 3 - i) % 4
            remote(dres.at[0], dret.at[src], dret_send.at[i], dret_recv.at[src], tp_peer[i]).wait_recv()
        top = dec_l[...]
        for q in range(4):
            top = jnp.maximum(top, dret[q, 1])
        w = jnp.exp2(dec_l[...] - top)
        num, den = w * dec_o[...], w
        for q in range(4):
            w = jnp.exp2(dret[q, 1] - top)
            num, den = num + w * dret[q, 0], den + w
        dec_ref[...] = (num / den).astype(BF)

    def core_copy(h):
        return remote(obuf.at[h, 1 - co], cbuf.at[h], core_send.at[h], core_recv.at[h], core_peer)

    def y_copy(h, i):
        return remote(
            obuf.at[h, co, (y + 1 + i) % 4], ybuf.at[h, y], y_send.at[h, i], y_recv.at[h, y], y_peer[i]
        )

    def finish_head(h):
        def body(g, carry):
            j = h * 8 + g
            o = (acc_ref[j] / l_ref[j]).T
            for k in range(8):
                obuf[h, k % 2, k // 2, g] = o[k * 32 : (k + 1) * 32]
            return carry

        lax.fori_loop(0, 8, body, 0)
        lse = [m_ref[h * 8 + g] + jnp.log2(l_ref[h * 8 + g]) for g in range(8)]
        lse = jnp.concatenate(lse + [jnp.zeros((120, ROWS), F32)], axis=0).T
        for k in range(8):
            obuf[h, k % 2, k // 2, 8] = lse[k * 32 : (k + 1) * 32]
        core_copy(h).start()

    def merge_cores(h):
        core_copy(h).wait_recv()

        def body(i, carry):
            a, b = obuf[h, co, i, 8], cbuf[h, i, 8]
            top = jnp.maximum(a, b)
            wa, wb = jnp.exp2(a - top), jnp.exp2(b - top)
            both = wa + wb
            obuf[h, co, i, 8] = top + jnp.log2(both)
            wa, wb = wa / both, wb / both
            for g in range(8):
                obuf[h, co, i, g] = obuf[h, co, i, g] * wa[:, g : g + 1] + cbuf[h, i, g] * wb[:, g : g + 1]
            return carry

        lax.fori_loop(0, 4, body, 0)
        for i in range(3):
            y_copy(h, i).start()

    def merge_y(h):
        for i in range(3):
            src = (y + 3 - i) % 4
            remote(
                obuf.at[h, co, 0], ybuf.at[h, src], y_send.at[h, i], y_recv.at[h, src], y_peer[i]
            ).wait_recv()
        ybuf[h, y] = obuf[h, co, y]
        parts = [ybuf[h, i, 8] for i in range(4)]
        top = functools.reduce(jnp.maximum, parts)
        w = [jnp.exp2(p - top) for p in parts]
        inv = 1.0 / (w[0] + w[1] + w[2] + w[3])
        w = [a * inv for a in w]
        for g in range(8):
            o = ybuf[h, 0, g] * w[0][:, g : g + 1]
            for i in range(1, 4):
                o = o + ybuf[h, i, g] * w[i][:, g : g + 1]
            out_ref[:, (h * 8 + g) * HEAD : (h * 8 + g + 1) * HEAD] = o.astype(BF)

    ahead = {k: [] for k in range(17)}
    ahead[1] += [pick_slot_share]
    ahead[2] += [decode_cache, lambda: arrive(0, L)]
    ahead[3] += [lambda: arrive(0, R), pass_small]
    ahead[4] += [lambda: arrive(0, O), lambda: arrive(0, Z)]
    ahead[5] += [lambda: arrive(1, L)]
    ahead[6] += [lambda: arrive(1, R)]
    ahead[8] += [lambda: arrive(0, ZL), lambda: arrive(0, ZR)]
    ahead[10] += [lambda: arrive(1, O), lambda: arrive(1, Z)]
    ahead[11] += [take_small, stretch_part, decode_stretch, lambda: arrive(0, ZO)]
    ahead[12] += [lambda: finish_head(0)]
    ahead[13] += [lambda: merge_cores(0), lambda: arrive(1, ZL)]
    ahead[14] += [lambda: arrive(1, ZR), decode_finish]
    ahead[15] += [lambda: arrive(1, ZO)]

    def step(n, carry):
        h = 0
        slot = 0
        for k, (hk, which) in enumerate(ORDER):
            if hk:
                h = h + jnp.where(n == k, 1, 0)
            slot = slot + jnp.where(n == k, slots[which], 0)
            if ahead[k]:

                def go(k=k):
                    for f in ahead[k]:
                        f()

                pl.when(n == k)(go)
        when(True if blocks >= 8 else slot < blocks, lambda: flash_block(h, slot))
        return carry

    lax.fori_loop(0, 16, step, 0)
    finish_head(1)
    merge_cores(1)
    merge_y(0)
    merge_y(1)

    def own_done():
        for h in range(2):
            for s in own_sends:
                make(h, s).wait_send()

    when(exists(OWN), own_done)
    for which, sends in forwards.items():

        def fwd_done(sends=sends):
            for h in range(2):
                for s in sends:
                    make(h, s).wait_send()

        when(exists(which), fwd_done)
    for n, to in enumerate((Z, L, R, O)):
        small_copy(OWN, to, n).wait_send()
    for n, to in enumerate((L, R, O)):
        small_copy(Z, to, 4 + n).wait_send()
    for cp in dret_copies:
        cp.wait_send()
    for h in range(2):
        core_copy(h).wait_send()
        for i in range(3):
            y_copy(h, i).wait_send()


def fused(blocks, args):
    vmem = pl.BlockSpec(memory_space=pltpu.VMEM)
    smem = pl.BlockSpec(memory_space=pltpu.SMEM)
    anym = pl.BlockSpec(memory_space=pl.ANY)
    dma = pltpu.SemaphoreType.DMA
    return pl.pallas_call(
        functools.partial(kernel, blocks),
        out_shape=(
            jax.ShapeDtypeStruct((32, 2048), BF),
            jax.ShapeDtypeStruct((64, HEAD), BF),
        ),
        in_specs=[smem] * 3 + [vmem] * 8 + [anym] * 2,
        out_specs=(vmem, vmem),
        scratch_shapes=[
            pltpu.VMEM((4, CACHE, HEAD), BF),
            pltpu.VMEM((4, CACHE, HEAD), BF),
            pltpu.VMEM((16, ROWS, 2 * HEAD), BF),
            pltpu.VMEM((2, 8, BLOCK, 2 * HEAD), BF),
            pltpu.VMEM((2, 8, HEAD, BLOCK), BF),
            pltpu.VMEM((8, 256, HEAD), BF),
            pltpu.VMEM((4, 2, 64, HEAD), BF),
            pltpu.VMEM((4, 2, 64, HEAD), BF),
            pltpu.VMEM((4, 64, HEAD), BF),
            pltpu.VMEM((2, ROWS, HEAD), BF),
            pltpu.VMEM((2, HEAD, ROWS), BF),
            pltpu.VMEM((HEAD, BLOCK), BF),
            pltpu.VMEM((4, 2, 64, HEAD), F32),
            pltpu.VMEM((4, 2, 64, HEAD), F32),
            pltpu.VMEM((64, HEAD), F32),
            pltpu.VMEM((64, HEAD), F32),
            pltpu.VMEM((2, BLOCK, ROWS), F32),
            pltpu.VMEM((2, BLOCK, ROWS), F32),
            pltpu.VMEM((2, 1, ROWS), F32),
            pltpu.VMEM((2, 1, ROWS), F32),
            pltpu.VMEM((16, 1, ROWS), F32),
            pltpu.VMEM((16, 1, ROWS), F32),
            pltpu.VMEM((16, HEAD, ROWS), F32),
            pltpu.VMEM((2, 2, 4, 9, 32, HEAD), F32),
            pltpu.VMEM((2, 4, 9, 32, HEAD), F32),
            pltpu.VMEM((2, 4, 9, 32, HEAD), F32),
            dma((4, 2)),
            dma((2, 14)),
            dma((2, 8, 2)),
            dma((7,)),
            dma((8,)),
            dma((3,)),
            dma((4,)),
            dma((3,)),
            dma((4,)),
            dma((3,)),
            dma((4,)),
            dma((2,)),
            dma((2,)),
            dma((2, 3)),
            dma((2, 4)),
        ],
        compiler_params=pltpu.CompilerParams(
            collective_id=blocks, has_side_effects=True, vmem_limit_bytes=56 << 20
        ),
        name=f"attention_{blocks}",
    )(*args)


def shards(
    stretch_query_rows,
    stretch_key_rows,
    stretch_value_rows,
    prefix_key_rows,
    prefix_value_rows,
    offset,
    decode_query_rows,
    decode_keys,
    decode_value_rows,
    cache_keys,
    cached_value_rows,
    cache_lengths,
    head_slot_index,
):
    dq = decode_query_rows.reshape(2, 4, GROUP, HEAD).transpose(1, 0, 2, 3).reshape(64, HEAD)
    args = (
        offset,
        head_slot_index,
        cache_lengths,
        stretch_query_rows,
        prefix_key_rows,
        prefix_value_rows,
        stretch_key_rows,
        stretch_value_rows,
        dq,
        decode_keys.reshape(8, HEAD),
        decode_value_rows.reshape(8, HEAD),
        cache_keys.reshape(4, CACHE, HEAD),
        cached_value_rows.reshape(4, CACHE, HEAD),
    )
    prefill_out, dec = fused(8, args)
    decode_output = dec.reshape(4, 2, GROUP, HEAD).transpose(1, 0, 2, 3).reshape(2, 4, 1, GROUP * HEAD)
    return prefill_out, decode_output


def solution(mesh):
    placed = (
        P("ctx", "tp"),
        P("ctx", "tp"),
        P("ctx", "tp"),
        P(("ctx", "dec"), "tp"),
        P(("ctx", "dec"), "tp"),
        P(),
        P(None, ("ctx", "tp"), "dec", None),
        P(None, ("ctx", "tp"), "dec", None),
        P(None, ("ctx", "tp"), "dec", None),
        P(("ctx", "tp"), "dec", None, None),
        P(("ctx", "tp"), "dec", None, None),
        P(("ctx", "tp")),
        P(),
    )
    return jax.shard_map(
        shards,
        mesh=mesh,
        in_specs=placed,
        out_specs=(P(("ctx", "dec"), "tp"), P(None, ("ctx", "tp"), "dec", None)),
        check_vma=False,
    )
```

time: 582 us -> 111 us (0.19)
  the two profiles are of different devices: /device:TPU:1 before, /device:TPU:33 now
where the time goes in v1:
time: 111 us
  Pallas kernels  105 us (95%)
  local copies, waits for them, and re-layouts  4.25 us (4%)
  between operations  1.29 us (1%)
    pallas_call x1, Pallas kernels, fused(): pl.pallas_call(functools.partial(kernel, blocks), out_shape=(jax.ShapeDty...  105 us

profile of v1, /device:TPU:33, one launch (start us, length us, event | category | flops | bytes accessed | tf_op | source)
XLA Modules:
  0.0 111.0 jit_solution(950724662998742437)
XLA Ops:
  1.3 0.7 reshape.28
  2.0 0.6 copy.15
  2.6 105.5 %attention_8.1 = (bf16[32,2048]{1,0:T(8,128)(2,1)}, bf16[64,128]{1,0:T(8,128)(2,1)}) custom-call(s32[1]{0:T(128)S(6)} %copy.19.offset_ref, s32[8]{0:T(128)} %slot_index_ref.1, s32[4]{0:T(128)} %lengths_ref.1, bf16[256,2048]{1,0:T(8,128)(2,1)} %q_ref.1, bf16[512,256]{1,0:T(8,128)(2,1)} %pk_ref.1, bf16[512,256]{1,0:T(8,128)(2,1)} %pv_ref.1, ...), custom_call_target="tpu_custom_call" | custom-call | tf_op jit(solution)/shard_map/attention_8/pallas_call | solution.py:527
  108.1 0.7 reshape.36
  108.8 0.6 copy.17
  109.4 1.6 %copy.20 = bf16[32,2048]{1,0:T(8,128)(2,1)} copy(bf16[32,2048]{1,0:T(8,128)(2,1)} %get-tuple-element.8) | data formatting | bytes 262144

commit v2 on v1

--- a/solution.py
+++ b/solution.py
@@ -25,15 +25,15 @@
     (1, OWN),
     (0, L),
     (0, R),
-    (0, O),
     (1, L),
     (1, R),
     (0, Z),
+    (0, O),
+    (1, O),
+    (1, Z),
     (0, ZL),
     (0, ZR),
-    (1, O),
     (0, ZO),
-    (1, Z),
     (1, ZL),
     (1, ZR),
     (1, ZO),
@@ -75,9 +75,11 @@
     qx,
     kbuf,
     vbuf,
-    small,
+    share,
+    slot_rows,
     cand,
     scat,
+    dq_rows,
     dqall,
     kst,
     vst,
@@ -99,8 +101,10 @@
     cache_sem,
     send_sem,
     recv_sem,
-    small_send,
-    small_recv,
+    share_send,
+    share_recv,
+    slot_send,
+    slot_recv,
     scat_send,
     scat_recv,
     dq_send,
@@ -189,9 +193,14 @@
             cand[q, i] = chosen[q * 64 : (q + 1) * 64]
         mine = pl.ds(pl.multiple_of(d * 32, 32), 32)
         for h in range(2):
-            small[me, (2 * i + h) * 32 : (2 * i + h + 1) * 32, :] = ref[mine, h * HEAD : (h + 1) * HEAD]
+            share[me, (2 * i + h) * 32 : (2 * i + h + 1) * 32, :] = ref[mine, h * HEAD : (h + 1) * HEAD]
     scat[t] = cand[t]
-    dqall[t] = dq_ref[...]
+    for u in range(2):
+        wide = dq_ref[u].astype(F32)
+        for g in range(GROUP):
+            at = (u * GROUP + g) * 4
+            dq_rows[at : at + 4, :] = wide[:, g * HEAD : (g + 1) * HEAD]
+    dqall[t] = dq_rows[...].astype(BF)
 
     pl.semaphore_wait(barrier, len(peers))
 
@@ -222,27 +231,60 @@
         for s in sends:
             make(h, s).start()
 
+    def arrive_one(h, which, kv):
+        def go():
+            (copy_v if kv else copy_k)(h, which, L, 0).wait_recv()
+            start_all(h, [f for f in forwards.get(which, []) if f[1] == kv])
+
+        when(exists(which), go)
+
     def arrive(h, which):
-        def go():
-            copy_k(h, which, L, 0).wait_recv()
-            copy_v(h, which, L, 0).wait_recv()
-            start_all(h, forwards.get(which, []))
-
-        when(exists(which), go)
-
-    for h in range(2):
-        when(exists(OWN), functools.partial(start_all, h, own_sends))
-        if h == 0:
-            scat_copies = []
-            dq_copies = []
-            for i in range(3):
-                q = (t + 1 + i) % 4
-                cp = remote(cand.at[q], scat.at[t], scat_send.at[i], scat_recv.at[t], tp_peer[i])
-                cp.start()
-                scat_copies.append(cp)
-                cp = remote(dqall.at[t], dqall.at[t], dq_send.at[i], dq_recv.at[t], tp_peer[i])
-                cp.start()
-                dq_copies.append(cp)
+        arrive_one(h, which, 0)
+        arrive_one(h, which, 1)
+
+    def share_copy(buf, ss, rs, which, to, n):
+        ref = buf.at[slots[which]]
+        return remote(ref, ref, ss.at[n], rs.at[slots[which]], dev[to])
+
+    stretch_share = functools.partial(share_copy, share, share_send, share_recv)
+    slot_share = functools.partial(share_copy, slot_rows, slot_send, slot_recv)
+
+    def send_share(copy):
+        for n, to in enumerate((Z, L, R, O)):
+            copy(OWN, to, n).start()
+
+    def pass_share(copy):
+        copy(Z, L, 0).wait_recv()
+        for n, to in enumerate((L, R, O)):
+            copy(Z, to, 4 + n).start()
+
+    def take_share(copy):
+        for which in (L, R, O, ZL, ZR, ZO):
+            copy(which, L, 0).wait_recv()
+
+    def share_done(copy):
+        for n, to in enumerate((Z, L, R, O)):
+            copy(OWN, to, n).wait_send()
+        for n, to in enumerate((L, R, O)):
+            copy(Z, to, 4 + n).wait_send()
+
+    scat_copies = []
+    dq_copies = []
+    for i in range(3):
+        q = (t + 1 + i) % 4
+        cp = remote(cand.at[q], scat.at[t], scat_send.at[i], scat_recv.at[t], tp_peer[i])
+        cp.start()
+        scat_copies.append(cp)
+        cp = remote(dqall.at[t], dqall.at[t], dq_send.at[i], dq_recv.at[t], tp_peer[i])
+        cp.start()
+        dq_copies.append(cp)
+
+    def start_own():
+        start_all(0, own_sends)
+        start_all(1, own_sends)
+
+    send_share(stretch_share)
+    when(exists(OWN), start_own)
 
     one_lane = (lax.broadcasted_iota(jnp.int32, (ROWS, HEAD), 1) == 0).astype(F32).astype(BF)
     for j in range(16):
@@ -275,20 +317,13 @@
 
     def flash_block(h, slot):
         score(h, slot, 0, s_a, x_a)
-
-        def body(i, carry):
-            g = 2 * i
-            score(h, slot, g + 1, s_b, x_b)
-            absorb(h, slot, g, s_a, x_a)
-            score(h, slot, jnp.minimum(g + 2, 3), s_a, x_a)
-            absorb(h, slot, g + 1, s_b, x_b)
-            return carry
-
-        lax.fori_loop(0, 2, body, 0)
-
-    def small_copy(which, to, n):
-        ref = small.at[slots[which]]
-        return remote(ref, ref, small_send.at[n], small_recv.at[slots[which]], dev[to])
+        score(h, slot, 1, s_b, x_b)
+        absorb(h, slot, 0, s_a, x_a)
+        score(h, slot, 2, s_a, x_a)
+        absorb(h, slot, 1, s_b, x_b)
+        score(h, slot, 3, s_b, x_b)
+        absorb(h, slot, 2, s_a, x_a)
+        absorb(h, slot, 3, s_b, x_b)
 
     def pick_slot_share():
         for cp in dq_copies + scat_copies:
@@ -298,54 +333,56 @@
             remote(cand.at[0], scat.at[src], scat_send.at[i], scat_recv.at[src], tp_peer[i]).wait_recv()
         source = my_head // 2
         for i in range(2):
-            share = scat[0, i]
+            quarter = scat[0, i]
             for q in range(1, 4):
-                share = jnp.where(source == q, scat[q, i], share)
-            small[me, 128 + 64 * i : 192 + 64 * i, :] = share
-        for n, to in enumerate((Z, L, R, O)):
-            small_copy(OWN, to, n).start()
-
-    def pass_small():
-        small_copy(Z, L, 0).wait_recv()
-        for n, to in enumerate((L, R, O)):
-            small_copy(Z, to, 4 + n).start()
-
-    def take_small():
-        for which in (L, R, O, ZL, ZR, ZO):
-            small_copy(which, L, 0).wait_recv()
+                quarter = jnp.where(source == q, scat[q, i], quarter)
+            slot_rows[me, 64 * i : 64 * i + 64, :] = quarter
+        send_share(slot_share)
+
+    def stretch_part():
+        take_share(stretch_share)
         for h in range(2):
-            kst[h] = small[:, h * 32 : (h + 1) * 32, :].reshape(ROWS, HEAD)
-            vst[h] = small[:, 64 + h * 32 : 96 + h * 32, :].reshape(ROWS, HEAD).T
-        vslot[...] = small[:, 192:256, :].reshape(BLOCK, HEAD).T
-
-    def stretch_part():
+            kst[h] = share[:, h * 32 : (h + 1) * 32, :].reshape(ROWS, HEAD)
+            vst[h] = share[:, 64 + h * 32 : 96 + h * 32, :].reshape(ROWS, HEAD).T
         kk = lax.broadcasted_iota(jnp.int32, (ROWS, ROWS), 0)
         key_row = (kk // 32) * ROWS + d * 32 + kk % 32
         query_row = c * ROWS + lax.broadcasted_iota(jnp.int32, (ROWS, ROWS), 1)
         usable = key_row <= query_row
 
-        def body(i, carry):
-            h = i // 4
+        def stretch_score(h, g, s_ref, x_ref):
             for u in range(2):
-                j = 2 * i + u
-                s = jnp.where(usable, nt_dot(kst[h], qx[j, :, :HEAD]), NEG)
-                update(j, s, jnp.max(s, axis=0, keepdims=True) * SCALE, vst[h])
+                s = jnp.where(usable, nt_dot(kst[h], qx[h * 8 + g * 2 + u, :, :HEAD]), NEG)
+                s_ref[u, :ROWS] = s
+                x_ref[u] = jnp.max(s, axis=0, keepdims=True) * SCALE
+
+        def stretch_absorb(h, g, s_ref, x_ref):
+            for u in range(2):
+                update(h * 8 + g * 2 + u, s_ref[u, :ROWS], x_ref[u], vst[h])
+
+        def body(h, carry):
+            stretch_score(h, 0, s_a, x_a)
+            stretch_score(h, 1, s_b, x_b)
+            stretch_absorb(h, 0, s_a, x_a)
+            stretch_score(h, 2, s_a, x_a)
+            stretch_absorb(h, 1, s_b, x_b)
+            stretch_score(h, 3, s_b, x_b)
+            stretch_absorb(h, 2, s_a, x_a)
+            stretch_absorb(h, 3, s_b, x_b)
             return carry
 
-        lax.fori_loop(0, 8, body, 0)
+        lax.fori_loop(0, 2, body, 0)
 
     def decode_cache():
         for cp in cache_copies:
             cp.wait()
         step_row = lax.broadcasted_iota(jnp.int32, (16, 1), 0) >= 8
         for r in range(4):
-            q = dq_ref[r * 16 : (r + 1) * 16, :]
-            qf = q.astype(F32)
-            s = nt_dot(q, ck[r]) * SCALE
+            qf = dq_rows[pl.ds(r, 16, stride=4), :]
+            s = nt_dot(qf.astype(BF), ck[r]) * SCALE
             s = jnp.where(lax.broadcasted_iota(jnp.int32, (16, CACHE), 1) < lengths_ref[r], s, NEG)
             new = []
             for u in range(2):
-                sn = jnp.sum(qf * dk_ref[u * 4 + r : u * 4 + r + 1, :].astype(F32), axis=1, keepdims=True) * SCALE
+                sn = jnp.sum(qf * dk_ref[u].astype(F32)[r : r + 1, :], axis=1, keepdims=True) * SCALE
                 new.append(jnp.where(step_row, sn, NEG) if u else sn)
             top = jnp.maximum(jnp.max(s, axis=1, keepdims=True), jnp.maximum(new[0], new[1]))
             p = jnp.exp2(s - top)
@@ -355,19 +392,21 @@
             mixed = dot(jnp.concatenate([hi, lo], axis=0), cv[r])
             mixed = mixed[:16] + mixed[16:]
             for u in range(2):
-                mixed = mixed + pn[u] * dv_ref[u * 4 + r : u * 4 + r + 1, :].astype(F32)
-            dec_o[r * 16 : (r + 1) * 16, :] = mixed / total
-            dec_l[r * 16 : (r + 1) * 16, :] = jnp.broadcast_to(top + jnp.log2(total), (16, HEAD))
+                mixed = mixed + pn[u] * dv_ref[u].astype(F32)[r : r + 1, :]
+            dec_o[pl.ds(r, 16, stride=4), :] = mixed / total
+            dec_l[pl.ds(r, 16, stride=4), :] = jnp.broadcast_to(top + jnp.log2(total), (16, HEAD))
 
     dret_copies = [
         remote(dres.at[(t + 1 + i) % 4], dret.at[t], dret_send.at[i], dret_recv.at[t], tp_peer[i]) for i in range(3)
     ]
 
     def decode_stretch():
+        take_share(slot_share)
+        vslot[...] = slot_rows[:, 64:128, :].reshape(BLOCK, HEAD).T
         for i in range(3):
             src = (t + 3 - i) % 4
             remote(dqall.at[src], dqall.at[src], dq_send.at[i], dq_recv.at[src], tp_peer[i]).wait_recv()
-        keys = small[:, 128:192, :].reshape(BLOCK, HEAD)
+        keys = slot_rows[:, 0:64, :].reshape(BLOCK, HEAD)
         s = nt_dot(keys, dqall[...].reshape(4 * 64, HEAD)) * SCALE
         top = jnp.max(s, axis=0, keepdims=True)
         p = jnp.exp2(s - top)
@@ -394,7 +433,11 @@
         for q in range(4):
             w = jnp.exp2(dret[q, 1] - top)
             num, den = num + w * dret[q, 0], den + w
-        dec_ref[...] = (num / den).astype(BF)
+        res = num / den
+        for u in range(2):
+            for g in range(GROUP):
+                at = (u * GROUP + g) * 4
+                dec_ref[u, :, g * HEAD : (g + 1) * HEAD] = res[at : at + 4, :].astype(BF)
 
     def core_copy(h):
         return remote(obuf.at[h, 1 - co], cbuf.at[h], core_send.at[h], core_recv.at[h], core_peer)
@@ -455,19 +498,19 @@
                 o = o + ybuf[h, i, g] * w[i][:, g : g + 1]
             out_ref[:, (h * 8 + g) * HEAD : (h * 8 + g + 1) * HEAD] = o.astype(BF)
 
-    ahead = {k: [] for k in range(17)}
-    ahead[1] += [pick_slot_share]
-    ahead[2] += [decode_cache, lambda: arrive(0, L)]
-    ahead[3] += [lambda: arrive(0, R), pass_small]
-    ahead[4] += [lambda: arrive(0, O), lambda: arrive(0, Z)]
-    ahead[5] += [lambda: arrive(1, L)]
-    ahead[6] += [lambda: arrive(1, R)]
-    ahead[8] += [lambda: arrive(0, ZL), lambda: arrive(0, ZR)]
-    ahead[10] += [lambda: arrive(1, O), lambda: arrive(1, Z)]
-    ahead[11] += [take_small, stretch_part, decode_stretch, lambda: arrive(0, ZO)]
-    ahead[12] += [lambda: finish_head(0)]
-    ahead[13] += [lambda: merge_cores(0), lambda: arrive(1, ZL)]
-    ahead[14] += [lambda: arrive(1, ZR), decode_finish]
+    ahead = {k: [] for k in range(16)}
+    ahead[2] += [lambda: arrive(0, L), lambda: arrive(0, R)]
+    ahead[4] += [decode_cache, lambda: arrive(1, L), lambda: arrive(1, R), lambda: arrive_one(0, Z, 0)]
+    ahead[5] += [lambda: arrive_one(0, Z, 1)]
+    ahead[6] += [pick_slot_share, lambda: pass_share(stretch_share)]
+    ahead[7] += [lambda: arrive(0, O)]
+    ahead[8] += [lambda: arrive_one(1, Z, 0), lambda: arrive(1, O)]
+    ahead[9] += [lambda: arrive_one(1, Z, 1)]
+    ahead[10] += [lambda: arrive(0, ZL), lambda: arrive(0, ZR)]
+    ahead[11] += [lambda: pass_share(slot_share)]
+    ahead[12] += [stretch_part, lambda: arrive(0, ZO)]
+    ahead[13] += [lambda: arrive(1, ZL), lambda: arrive(1, ZR), lambda: finish_head(0)]
+    ahead[14] += [lambda: merge_cores(0)]
     ahead[15] += [lambda: arrive(1, ZO)]
 
     def step(n, carry):
@@ -489,8 +532,10 @@
 
     lax.fori_loop(0, 16, step, 0)
     finish_head(1)
+    decode_stretch()
     merge_cores(1)
     merge_y(0)
+    decode_finish()
     merge_y(1)
 
     def own_done():
@@ -507,10 +552,8 @@
                     make(h, s).wait_send()
 
         when(exists(which), fwd_done)
-    for n, to in enumerate((Z, L, R, O)):
-        small_copy(OWN, to, n).wait_send()
-    for n, to in enumerate((L, R, O)):
-        small_copy(Z, to, 4 + n).wait_send()
+    share_done(stretch_share)
+    share_done(slot_share)
     for cp in dret_copies:
         cp.wait_send()
     for h in range(2):
@@ -528,7 +571,7 @@
         functools.partial(kernel, blocks),
         out_shape=(
             jax.ShapeDtypeStruct((32, 2048), BF),
-            jax.ShapeDtypeStruct((64, HEAD), BF),
+            jax.ShapeDtypeStruct((2, 4, GROUP * HEAD), BF),
         ),
         in_specs=[smem] * 3 + [vmem] * 8 + [anym] * 2,
         out_specs=(vmem, vmem),
@@ -538,9 +581,11 @@
             pltpu.VMEM((16, ROWS, 2 * HEAD), BF),
             pltpu.VMEM((2, 8, BLOCK, 2 * HEAD), BF),
             pltpu.VMEM((2, 8, HEAD, BLOCK), BF),
-            pltpu.VMEM((8, 256, HEAD), BF),
+            pltpu.VMEM((8, 128, HEAD), BF),
+            pltpu.VMEM((8, 128, HEAD), BF),
             pltpu.VMEM((4, 2, 64, HEAD), BF),
             pltpu.VMEM((4, 2, 64, HEAD), BF),
+            pltpu.VMEM((64, HEAD), F32),
             pltpu.VMEM((4, 64, HEAD), BF),
             pltpu.VMEM((2, ROWS, HEAD), BF),
             pltpu.VMEM((2, HEAD, ROWS), BF),
@@ -564,6 +609,8 @@
             dma((2, 8, 2)),
             dma((7,)),
             dma((8,)),
+            dma((7,)),
+            dma((8,)),
             dma((3,)),
             dma((4,)),
             dma((3,)),
@@ -597,7 +644,6 @@
     cache_lengths,
     head_slot_index,
 ):
-    dq = decode_query_rows.reshape(2, 4, GROUP, HEAD).transpose(1, 0, 2, 3).reshape(64, HEAD)
     args = (
         offset,
         head_slot_index,
@@ -607,15 +653,14 @@
         prefix_value_rows,
         stretch_key_rows,
         stretch_value_rows,
-        dq,
-        decode_keys.reshape(8, HEAD),
-        decode_value_rows.reshape(8, HEAD),
+        decode_query_rows.reshape(2, 4, GROUP * HEAD),
+        decode_keys.reshape(2, 4, HEAD),
+        decode_value_rows.reshape(2, 4, HEAD),
         cache_keys.reshape(4, CACHE, HEAD),
         cached_value_rows.reshape(4, CACHE, HEAD),
     )
     prefill_out, dec = fused(8, args)
-    decode_output = dec.reshape(4, 2, GROUP, HEAD).transpose(1, 0, 2, 3).reshape(2, 4, 1, GROUP * HEAD)
-    return prefill_out, decode_output
+    return prefill_out, dec.reshape(2, 4, 1, GROUP * HEAD)
 
 
 def solution(mesh):

time: 111 us -> 87 us (0.78)
  the two profiles are of different devices: /device:TPU:33 before, /device:TPU:1 now
where the time goes in v2:
time: 87 us; the launch traced here: 86.6 us
  Pallas kernels  82.4 us (95%)
  local copies, waits for them, and re-layouts  2.9 us (3%)
  between operations  1.29 us (1%)
    pallas_call x1, Pallas kernels, fused(): pl.pallas_call(functools.partial(kernel, blocks), out_shape=(jax.ShapeDty...  82.4 us
    unnamed x2, local copies, waits for them, and re-layouts  2.9 us

profile of v2, /device:TPU:1, one launch (start us, length us, event | category | flops | bytes accessed | tf_op | source)
XLA Modules:
  0.0 86.6 jit_solution(18156507398566085345)
XLA Ops:
  1.3 82.4 %attention_8.1 = (bf16[32,2048]{1,0:T(8,128)(2,1)}, bf16[2,4,1024]{2,1,0:T(4,128)(2,1)}) custom-call(s32[1]{0:T(128)S(6)} %copy.18.offset_ref, s32[8]{0:T(128)} %slot_index_ref.1, s32[4]{0:T(128)} %lengths_ref.1, bf16[256,2048]{1,0:T(8,128)(2,1)} %q_ref.1, bf16[512,256]{1,0:T(8,128)(2,1)} %pk_ref.1, bf16[512,256]{1,0:T(8,128)(2,1)} %pv_ref.1, ...), custom_call_target="tpu_custom_call" | custom-call | tf_op jit(solution)/shard_map/attention_8/pallas_call | solution.py:570
  83.7 1.6 %copy.19 = bf16[32,2048]{1,0:T(8,128)(2,1)} copy(bf16[32,2048]{1,0:T(8,128)(2,1)} %get-tuple-element.10) | data formatting | bytes 262144
  85.3 1.3 %copy.20 = bf16[2,4,1,1024]{3,1,2,0:T(4,128)(2,1)} copy(bf16[2,4,1,1024]{3,1,2,0:T(4,128)(2,1)} %bitcast.11) | data formatting | bytes 32768

commit v3 on v2

--- a/solution.py
+++ b/solution.py
@@ -20,23 +20,24 @@
 MESH = pl.DeviceIdType.MESH
 
 OWN, L, R, O, Z, ZL, ZR, ZO = range(8)
+MINE, PAIR = range(2)
 ORDER = [
-    (0, OWN),
-    (1, OWN),
-    (0, L),
-    (0, R),
-    (1, L),
-    (1, R),
-    (0, Z),
-    (0, O),
-    (1, O),
-    (1, Z),
-    (0, ZL),
-    (0, ZR),
-    (0, ZO),
-    (1, ZL),
-    (1, ZR),
-    (1, ZO),
+    (1, OWN, MINE),
+    (0, OWN, MINE),
+    (1, L, MINE),
+    (1, R, MINE),
+    (1, OWN, PAIR),
+    (1, L, PAIR),
+    (1, R, PAIR),
+    (1, O, MINE),
+    (1, O, PAIR),
+    (0, L, MINE),
+    (0, R, MINE),
+    (0, O, MINE),
+    (0, Z, MINE),
+    (0, ZL, MINE),
+    (0, ZR, MINE),
+    (0, ZO, MINE),
 ]
 
 
@@ -75,6 +76,8 @@
     qx,
     kbuf,
     vbuf,
+    q_pair,
+    q_all,
     share,
     slot_rows,
     cand,
@@ -98,6 +101,7 @@
     obuf,
     cbuf,
     ybuf,
+    zbuf,
     cache_sem,
     send_sem,
     recv_sem,
@@ -115,6 +119,10 @@
     core_recv,
     y_send,
     y_recv,
+    pair_sem,
+    q_send,
+    q_recv,
+    back_sem,
 ):
     c = lax.axis_index("ctx")
     t = lax.axis_index("tp")
@@ -139,6 +147,7 @@
     tp_peer = [(c, (t + i) % 4, d) for i in (1, 2, 3)]
     core_peer = (c, t, y * 2 + 1 - co)
     y_peer = [(c, t, ((y + i) % 4) * 2 + co) for i in (1, 2, 3)]
+    dec_peer = [(c, t, (d + i) % 8) for i in range(1, 8)]
 
     def remote(src, dst, ss, rs, to):
         return pltpu.make_async_remote_copy(
@@ -174,7 +183,7 @@
     lax.fori_loop(0, blocks, fill, 0)
 
     barrier = pltpu.get_barrier_semaphore()
-    peers = [dev[L], dev[R], dev[O], dev[Z], *tp_peer, core_peer, *y_peer]
+    peers = [dev[L], dev[R], dev[O], dev[Z], *tp_peer, *dec_peer]
     for p in peers:
         pl.semaphore_signal(barrier, inc=1, device_id=p, device_id_type=MESH)
 
@@ -214,7 +223,8 @@
         ref = vbuf.at[h, s]
         return remote(ref, ref, send_sem.at[h, n], recv_sem.at[h, s, 1], dev[to])
 
-    own_sends = [(OWN, 0, Z, 0), (OWN, 0, L, 1), (OWN, 0, R, 2), (OWN, 1, Z, 3), (OWN, 1, L, 4), (OWN, 1, R, 5)]
+    pair_sends = [(OWN, 0, Z, 0), (OWN, 1, Z, 3)]
+    x_sends = [(OWN, 0, L, 1), (OWN, 0, R, 2), (OWN, 1, L, 4), (OWN, 1, R, 5)]
     z_sends = [(Z, 0, L, 6), (Z, 0, R, 7), (Z, 1, L, 8), (Z, 1, R, 9)]
     forwards = {
         L: [(L, 0, R, 10)],
@@ -279,25 +289,43 @@
         cp.start()
         dq_copies.append(cp)
 
-    def start_own():
-        start_all(0, own_sends)
-        start_all(1, own_sends)
-
+    q_rows = pl.ds(pl.multiple_of(d * 32, 32), 32)
+    pair_copy = remote(q_ref.at[q_rows, pl.ds(8 * HEAD, 8 * HEAD)], q_pair, pair_sem.at[0], pair_sem.at[1], dev[Z])
+    pair_copy.start()
+    start_all(0, pair_sends)
+    start_all(1, x_sends)
+    start_all(0, x_sends)
     send_share(stretch_share)
-    when(exists(OWN), start_own)
+
+    def q_copy(i):
+        return remote(q_pair, q_all.at[d], q_send.at[i], q_recv.at[d], dec_peer[i])
+
+    def spread_queries():
+        pair_copy.wait_recv()
+        for i in range(7):
+            q_copy(i).start()
+        q_all[d] = q_pair[...]
+
+    def take_queries():
+        for i in range(7):
+            src = (d + 7 - i) % 8
+            remote(q_pair, q_all.at[src], q_send.at[i], q_recv.at[src], dec_peer[i]).wait_recv()
+        for g in range(8):
+            qx[16 + g, :, :HEAD] = q_all[:, :, g * HEAD : (g + 1) * HEAD].reshape(ROWS, HEAD)
 
     one_lane = (lax.broadcasted_iota(jnp.int32, (ROWS, HEAD), 1) == 0).astype(F32).astype(BF)
-    for j in range(16):
-        qx[j, :, :HEAD] = q_ref[:, j * HEAD : (j + 1) * HEAD]
+    for j in range(24):
+        if j < 16:
+            qx[j, :, :HEAD] = q_ref[:, j * HEAD : (j + 1) * HEAD]
         qx[j, :, HEAD:] = one_lane
     m_ref[...] = jnp.full(m_ref.shape, NEG, F32)
     l_ref[...] = jnp.zeros(l_ref.shape, F32)
     acc_ref[...] = jnp.zeros(acc_ref.shape, F32)
 
-    def score(h, slot, g, s_ref, x_ref):
+    def score(h, slot, base, g, s_ref, x_ref):
         keys = kbuf[h, slot]
         for u in range(2):
-            s = nt_dot(keys, qx[h * 8 + g * 2 + u])
+            s = nt_dot(keys, qx[base + g * 2 + u])
             s_ref[u] = s
             x_ref[u] = jnp.max(s, axis=0, keepdims=True) * SCALE
 
@@ -311,19 +339,19 @@
         hi, lo = split(p)
         acc_ref[j] = acc_ref[j] * fade + (dot(vt, hi) + dot(vt, lo))
 
-    def absorb(h, slot, g, s_ref, x_ref):
+    def absorb(h, slot, base, g, s_ref, x_ref):
         for u in range(2):
-            update(h * 8 + g * 2 + u, s_ref[u], x_ref[u], vbuf[h, slot])
-
-    def flash_block(h, slot):
-        score(h, slot, 0, s_a, x_a)
-        score(h, slot, 1, s_b, x_b)
-        absorb(h, slot, 0, s_a, x_a)
-        score(h, slot, 2, s_a, x_a)
-        absorb(h, slot, 1, s_b, x_b)
-        score(h, slot, 3, s_b, x_b)
-        absorb(h, slot, 2, s_a, x_a)
-        absorb(h, slot, 3, s_b, x_b)
+            update(base + g * 2 + u, s_ref[u], x_ref[u], vbuf[h, slot])
+
+    def flash_block(h, slot, base):
+        score(h, slot, base, 0, s_a, x_a)
+        score(h, slot, base, 1, s_b, x_b)
+        absorb(h, slot, base, 0, s_a, x_a)
+        score(h, slot, base, 2, s_a, x_a)
+        absorb(h, slot, base, 1, s_b, x_b)
+        score(h, slot, base, 3, s_b, x_b)
+        absorb(h, slot, base, 2, s_a, x_a)
+        absorb(h, slot, base, 3, s_b, x_b)
 
     def pick_slot_share():
         for cp in dq_copies + scat_copies:
@@ -487,38 +515,52 @@
                 obuf.at[h, co, 0], ybuf.at[h, src], y_send.at[h, i], y_recv.at[h, src], y_peer[i]
             ).wait_recv()
         ybuf[h, y] = obuf[h, co, y]
-        parts = [ybuf[h, i, 8] for i in range(4)]
-        top = functools.reduce(jnp.maximum, parts)
-        w = [jnp.exp2(p - top) for p in parts]
-        inv = 1.0 / (w[0] + w[1] + w[2] + w[3])
+        parts = [ybuf.at[h, i] for i in range(4)]
+        if h == 1:
+            back_copy.wait_recv()
+            parts.append(zbuf.at[1])
+        lse = [p[8] for p in parts]
+        top = functools.reduce(jnp.maximum, lse)
+        w = [jnp.exp2(a - top) for a in lse]
+        total = functools.reduce(jnp.add, w)
+        inv = 1.0 / total
         w = [a * inv for a in w]
+        if h == 2:
+            zbuf[0, 8] = top + jnp.log2(total)
         for g in range(8):
-            o = ybuf[h, 0, g] * w[0][:, g : g + 1]
-            for i in range(1, 4):
-                o = o + ybuf[h, i, g] * w[i][:, g : g + 1]
+            o = functools.reduce(jnp.add, [p[g] * a[:, g : g + 1] for p, a in zip(parts, w)])
+            if h == 2:
+                zbuf[0, g] = o
+                continue
             out_ref[:, (h * 8 + g) * HEAD : (h * 8 + g + 1) * HEAD] = o.astype(BF)
 
+    back_copy = remote(zbuf.at[0], zbuf.at[1], back_sem.at[0], back_sem.at[1], dev[Z])
+
+    def send_back():
+        merge_y(2)
+        back_copy.start()
+
     ahead = {k: [] for k in range(16)}
-    ahead[2] += [lambda: arrive(0, L), lambda: arrive(0, R)]
-    ahead[4] += [decode_cache, lambda: arrive(1, L), lambda: arrive(1, R), lambda: arrive_one(0, Z, 0)]
-    ahead[5] += [lambda: arrive_one(0, Z, 1)]
-    ahead[6] += [pick_slot_share, lambda: pass_share(stretch_share)]
-    ahead[7] += [lambda: arrive(0, O)]
-    ahead[8] += [lambda: arrive_one(1, Z, 0), lambda: arrive(1, O)]
-    ahead[9] += [lambda: arrive_one(1, Z, 1)]
-    ahead[10] += [lambda: arrive(0, ZL), lambda: arrive(0, ZR)]
-    ahead[11] += [lambda: pass_share(slot_share)]
-    ahead[12] += [stretch_part, lambda: arrive(0, ZO)]
-    ahead[13] += [lambda: arrive(1, ZL), lambda: arrive(1, ZR), lambda: finish_head(0)]
-    ahead[14] += [lambda: merge_cores(0)]
-    ahead[15] += [lambda: arrive(1, ZO)]
+    ahead[2] += [lambda: arrive(1, L), lambda: arrive(1, R), spread_queries]
+    ahead[4] += [lambda: arrive(0, L), lambda: arrive(0, R), take_queries]
+    ahead[5] += [lambda: arrive_one(0, Z, 0)]
+    ahead[6] += [lambda: arrive_one(0, Z, 1), lambda: pass_share(stretch_share), pick_slot_share]
+    ahead[7] += [lambda: arrive(1, O)]
+    ahead[9] += [lambda: finish_head(2)]
+    ahead[10] += [lambda: merge_cores(2)]
+    ahead[11] += [lambda: arrive(0, ZL), lambda: arrive(0, ZR), lambda: arrive(0, O), stretch_part, lambda: finish_head(1)]
+    ahead[12] += [lambda: merge_cores(1), lambda: pass_share(slot_share)]
+    ahead[14] += [send_back]
+    ahead[15] += [lambda: arrive(0, ZO)]
 
     def step(n, carry):
         h = 0
         slot = 0
-        for k, (hk, which) in enumerate(ORDER):
+        base = 0
+        for k, (hk, which, rows) in enumerate(ORDER):
             if hk:
                 h = h + jnp.where(n == k, 1, 0)
+                base = base + jnp.where(n == k, 16 if rows == PAIR else 8, 0)
             slot = slot + jnp.where(n == k, slots[which], 0)
             if ahead[k]:
 
@@ -527,36 +569,34 @@
                         f()
 
                 pl.when(n == k)(go)
-        when(True if blocks >= 8 else slot < blocks, lambda: flash_block(h, slot))
+        flash_block(h, slot, base)
         return carry
 
     lax.fori_loop(0, 16, step, 0)
-    finish_head(1)
+    finish_head(0)
     decode_stretch()
-    merge_cores(1)
+    merge_cores(0)
+    decode_cache()
+    merge_y(1)
+    decode_finish()
     merge_y(0)
-    decode_finish()
-    merge_y(1)
-
-    def own_done():
-        for h in range(2):
-            for s in own_sends:
+
+    pair_copy.wait_send()
+    back_copy.wait_send()
+    for i in range(7):
+        q_copy(i).wait_send()
+    for h, sends in ((0, pair_sends), (0, x_sends), (1, x_sends)):
+        for s in sends:
+            make(h, s).wait_send()
+    for which, sends in forwards.items():
+        for h in range(2 if which in (L, R) else 1):
+            for s in sends:
                 make(h, s).wait_send()
-
-    when(exists(OWN), own_done)
-    for which, sends in forwards.items():
-
-        def fwd_done(sends=sends):
-            for h in range(2):
-                for s in sends:
-                    make(h, s).wait_send()
-
-        when(exists(which), fwd_done)
     share_done(stretch_share)
     share_done(slot_share)
     for cp in dret_copies:
         cp.wait_send()
-    for h in range(2):
+    for h in range(3):
         core_copy(h).wait_send()
         for i in range(3):
             y_copy(h, i).wait_send()
@@ -578,9 +618,11 @@
         scratch_shapes=[
             pltpu.VMEM((4, CACHE, HEAD), BF),
             pltpu.VMEM((4, CACHE, HEAD), BF),
-            pltpu.VMEM((16, ROWS, 2 * HEAD), BF),
+            pltpu.VMEM((24, ROWS, 2 * HEAD), BF),
             pltpu.VMEM((2, 8, BLOCK, 2 * HEAD), BF),
             pltpu.VMEM((2, 8, HEAD, BLOCK), BF),
+            pltpu.VMEM((32, 8 * HEAD), BF),
+            pltpu.VMEM((8, 32, 8 * HEAD), BF),
             pltpu.VMEM((8, 128, HEAD), BF),
             pltpu.VMEM((8, 128, HEAD), BF),
             pltpu.VMEM((4, 2, 64, HEAD), BF),
@@ -598,12 +640,13 @@
             pltpu.VMEM((2, BLOCK, ROWS), F32),
             pltpu.VMEM((2, 1, ROWS), F32),
             pltpu.VMEM((2, 1, ROWS), F32),
-            pltpu.VMEM((16, 1, ROWS), F32),
-            pltpu.VMEM((16, 1, ROWS), F32),
-            pltpu.VMEM((16, HEAD, ROWS), F32),
-            pltpu.VMEM((2, 2, 4, 9, 32, HEAD), F32),
-            pltpu.VMEM((2, 4, 9, 32, HEAD), F32),
-            pltpu.VMEM((2, 4, 9, 32, HEAD), F32),
+            pltpu.VMEM((24, 1, ROWS), F32),
+            pltpu.VMEM((24, 1, ROWS), F32),
+            pltpu.VMEM((24, HEAD, ROWS), F32),
+            pltpu.VMEM((3, 2, 4, 9, 32, HEAD), F32),
+            pltpu.VMEM((3, 4, 9, 32, HEAD), F32),
+            pltpu.VMEM((3, 4, 9, 32, HEAD), F32),
+            pltpu.VMEM((2, 9, 32, HEAD), F32),
             dma((4, 2)),
             dma((2, 14)),
             dma((2, 8, 2)),
@@ -617,10 +660,14 @@
             dma((4,)),
             dma((3,)),
             dma((4,)),
+            dma((3,)),
+            dma((3,)),
+            dma((3, 3)),
+            dma((3, 4)),
             dma((2,)),
+            dma((7,)),
+            dma((8,)),
             dma((2,)),
-            dma((2, 3)),
-            dma((2, 4)),
         ],
         compiler_params=pltpu.CompilerParams(
             collective_id=blocks, has_side_effects=True, vmem_limit_bytes=56 << 20

time: 87 us -> 82.8 us (0.952)
  Pallas kernels: 82.4 us -> 78.4 us
    pallas_call x1, Pallas kernels: 82.4 us -> 78.4 us  [fused(): pl.pallas_call(functools.partial(kernel, blocks), out_shape=(jax.ShapeDty...]
where the time goes in v3:
time: 82.8 us; the launch traced here: 82.6 us
  Pallas kernels  78.4 us (95%)
  local copies, waits for them, and re-layouts  2.9 us (4%)
  between operations  1.29 us (2%)
    pallas_call x1, Pallas kernels, fused(): pl.pallas_call(functools.partial(kernel, blocks), out_shape=(jax.ShapeDty...  78.4 us
    unnamed x2, local copies, waits for them, and re-layouts  2.9 us

profile of v3, /device:TPU:1, one launch (start us, length us, event | category | flops | bytes accessed | tf_op | source)
XLA Modules:
  0.0 82.6 jit_solution(8152111281780248682)
XLA Ops:
  1.3 78.4 %attention_8.1 = (bf16[32,2048]{1,0:T(8,128)(2,1)}, bf16[2,4,1024]{2,1,0:T(4,128)(2,1)}) custom-call(s32[1]{0:T(128)S(6)} %copy.18.offset_ref, s32[8]{0:T(128)} %slot_index_ref.1, s32[4]{0:T(128)} %lengths_ref.1, bf16[256,2048]{1,0:T(8,128)(2,1)} %q_ref.1, bf16[512,256]{1,0:T(8,128)(2,1)} %pk_ref.1, bf16[512,256]{1,0:T(8,128)(2,1)} %pv_ref.1, ...), custom_call_target="tpu_custom_call" | custom-call | tf_op jit(solution)/shard_map/attention_8/pallas_call | solution.py:610
  79.7 1.6 %copy.19 = bf16[32,2048]{1,0:T(8,128)(2,1)} copy(bf16[32,2048]{1,0:T(8,128)(2,1)} %get-tuple-element.10) | data formatting | bytes 262144
  81.3 1.3 %copy.20 = bf16[2,4,1,1024]{3,1,2,0:T(4,128)(2,1)} copy(bf16[2,4,1,1024]{3,1,2,0:T(4,128)(2,1)} %bitcast.11) | data formatting | bytes 32768

commit v4 on v3

--- a/solution.py
+++ b/solution.py
@@ -211,6 +211,15 @@
             dq_rows[at : at + 4, :] = wide[:, g * HEAD : (g + 1) * HEAD]
     dqall[t] = dq_rows[...].astype(BF)
 
+    one_lane = (lax.broadcasted_iota(jnp.int32, (ROWS, HEAD), 1) == 0).astype(F32).astype(BF)
+    for j in range(24):
+        if j < 16:
+            qx[j, :, :HEAD] = q_ref[:, j * HEAD : (j + 1) * HEAD]
+        qx[j, :, HEAD:] = one_lane
+    m_ref[...] = jnp.full(m_ref.shape, NEG, F32)
+    l_ref[...] = jnp.zeros(l_ref.shape, F32)
+    acc_ref[...] = jnp.zeros(acc_ref.shape, F32)
+
     pl.semaphore_wait(barrier, len(peers))
 
     def copy_k(h, which, to, n):
@@ -313,15 +322,6 @@
         for g in range(8):
             qx[16 + g, :, :HEAD] = q_all[:, :, g * HEAD : (g + 1) * HEAD].reshape(ROWS, HEAD)
 
-    one_lane = (lax.broadcasted_iota(jnp.int32, (ROWS, HEAD), 1) == 0).astype(F32).astype(BF)
-    for j in range(24):
-        if j < 16:
-            qx[j, :, :HEAD] = q_ref[:, j * HEAD : (j + 1) * HEAD]
-        qx[j, :, HEAD:] = one_lane
-    m_ref[...] = jnp.full(m_ref.shape, NEG, F32)
-    l_ref[...] = jnp.zeros(l_ref.shape, F32)
-    acc_ref[...] = jnp.zeros(acc_ref.shape, F32)
-
     def score(h, slot, base, g, s_ref, x_ref):
         keys = kbuf[h, slot]
         for u in range(2):
@@ -344,14 +344,22 @@
             update(base + g * 2 + u, s_ref[u], x_ref[u], vbuf[h, slot])
 
     def flash_block(h, slot, base):
-        score(h, slot, base, 0, s_a, x_a)
-        score(h, slot, base, 1, s_b, x_b)
-        absorb(h, slot, base, 0, s_a, x_a)
-        score(h, slot, base, 2, s_a, x_a)
-        absorb(h, slot, base, 1, s_b, x_b)
-        score(h, slot, base, 3, s_b, x_b)
-        absorb(h, slot, base, 2, s_a, x_a)
-        absorb(h, slot, base, 3, s_b, x_b)
+        def score_one(g):
+            s = nt_dot(kbuf[h, slot], qx[base + g])
+            s_ref, x_ref = (s_a, x_a) if g % 4 < 2 else (s_b, x_b)
+            s_ref[g % 2] = s
+            x_ref[g % 2] = jnp.max(s, axis=0, keepdims=True) * SCALE
+
+        def absorb_one(g):
+            s_ref, x_ref = (s_a, x_a) if g % 4 < 2 else (s_b, x_b)
+            update(base + g, s_ref[g % 2], x_ref[g % 2], vbuf[h, slot])
+
+        for g in range(3):
+            score_one(g)
+        for g in range(8):
+            absorb_one(g)
+            if g + 3 < 8:
+                score_one(g + 3)
 
     def pick_slot_share():
         for cp in dq_copies + scat_copies:

time: 82.8 us -> 79.8 us (0.964)
  Pallas kernels: 78.4 us -> 75.4 us
    pallas_call x1, Pallas kernels: 78.4 us -> 75.4 us  [fused(): pl.pallas_call(functools.partial(kernel, blocks), out_shape=(jax.ShapeDty...]
where the time goes in v4:
time: 79.8 us; the launch traced here: 79.6 us
  Pallas kernels  75.4 us (94%)
  local copies, waits for them, and re-layouts  2.9 us (4%)
  between operations  1.29 us (2%)
    pallas_call x1, Pallas kernels, fused(): pl.pallas_call(functools.partial(kernel, blocks), out_shape=(jax.ShapeDty...  75.4 us
    unnamed x2, local copies, waits for them, and re-layouts  2.9 us

profile of v4, /device:TPU:1, one launch (start us, length us, event | category | flops | bytes accessed | tf_op | source)
XLA Modules:
  0.0 79.6 jit_solution(5872629533240018594)
XLA Ops:
  1.3 75.4 %attention_8.1 = (bf16[32,2048]{1,0:T(8,128)(2,1)}, bf16[2,4,1024]{2,1,0:T(4,128)(2,1)}) custom-call(s32[1]{0:T(128)S(6)} %copy.18.offset_ref, s32[8]{0:T(128)} %slot_index_ref.1, s32[4]{0:T(128)} %lengths_ref.1, bf16[256,2048]{1,0:T(8,128)(2,1)} %q_ref.1, bf16[512,256]{1,0:T(8,128)(2,1)} %pk_ref.1, bf16[512,256]{1,0:T(8,128)(2,1)} %pv_ref.1, ...), custom_call_target="tpu_custom_call" | custom-call | tf_op jit(solution)/shard_map/attention_8/pallas_call | solution.py:618
  76.7 1.6 %copy.19 = bf16[32,2048]{1,0:T(8,128)(2,1)} copy(bf16[32,2048]{1,0:T(8,128)(2,1)} %get-tuple-element.10) | data formatting | bytes 262144
  78.2 1.3 %copy.20 = bf16[2,4,1,1024]{3,1,2,0:T(4,128)(2,1)} copy(bf16[2,4,1,1024]{3,1,2,0:T(4,128)(2,1)} %bitcast.11) | data formatting | bytes 32768

commit v5 on v4

--- a/solution.py
+++ b/solution.py
@@ -486,12 +486,12 @@
     def finish_head(h):
         def body(g, carry):
             j = h * 8 + g
-            o = (acc_ref[j] / l_ref[j]).T
+            o = (acc_ref[j] * (1.0 / l_ref[j])).T
             for k in range(8):
                 obuf[h, k % 2, k // 2, g] = o[k * 32 : (k + 1) * 32]
             return carry
 
-        lax.fori_loop(0, 8, body, 0)
+        lax.fori_loop(0, 8, body, 0, unroll=4)
         lse = [m_ref[h * 8 + g] + jnp.log2(l_ref[h * 8 + g]) for g in range(8)]
         lse = jnp.concatenate(lse + [jnp.zeros((120, ROWS), F32)], axis=0).T
         for k in range(8):
@@ -512,7 +512,7 @@
                 obuf[h, co, i, g] = obuf[h, co, i, g] * wa[:, g : g + 1] + cbuf[h, i, g] * wb[:, g : g + 1]
             return carry
 
-        lax.fori_loop(0, 4, body, 0)
+        lax.fori_loop(0, 4, body, 0, unroll=2)
         for i in range(3):
             y_copy(h, i).start()
 

time: 79.8 us -> 77.9 us (0.976)
  Pallas kernels: 75.4 us -> 73.6 us
    pallas_call x1, Pallas kernels: 75.4 us -> 73.6 us  [fused(): pl.pallas_call(functools.partial(kernel, blocks), out_shape=(jax.ShapeDty...]
where the time goes in v5:
time: 77.9 us; the launch traced here: 77.7 us
  Pallas kernels  73.6 us (94%)
  local copies, waits for them, and re-layouts  2.9 us (4%)
  between operations  1.29 us (2%)
    pallas_call x1, Pallas kernels, fused(): pl.pallas_call(functools.partial(kernel, blocks), out_shape=(jax.ShapeDty...  73.6 us
    unnamed x2, local copies, waits for them, and re-layouts  2.9 us

profile of v5, /device:TPU:1, one launch (start us, length us, event | category | flops | bytes accessed | tf_op | source)
XLA Modules:
  0.0 77.7 jit_solution(9519309358629298091)
XLA Ops:
  1.3 73.6 %attention_8.1 = (bf16[32,2048]{1,0:T(8,128)(2,1)}, bf16[2,4,1024]{2,1,0:T(4,128)(2,1)}) custom-call(s32[1]{0:T(128)S(6)} %copy.18.offset_ref, s32[8]{0:T(128)} %slot_index_ref.1, s32[4]{0:T(128)} %lengths_ref.1, bf16[256,2048]{1,0:T(8,128)(2,1)} %q_ref.1, bf16[512,256]{1,0:T(8,128)(2,1)} %pk_ref.1, bf16[512,256]{1,0:T(8,128)(2,1)} %pv_ref.1, ...), custom_call_target="tpu_custom_call" | custom-call | tf_op jit(solution)/shard_map/attention_8/pallas_call | solution.py:618
  74.8 1.6 %copy.19 = bf16[32,2048]{1,0:T(8,128)(2,1)} copy(bf16[32,2048]{1,0:T(8,128)(2,1)} %get-tuple-element.10) | data formatting | bytes 262144
  76.4 1.3 %copy.20 = bf16[2,4,1,1024]{3,1,2,0:T(4,128)(2,1)} copy(bf16[2,4,1,1024]{3,1,2,0:T(4,128)(2,1)} %bitcast.11) | data formatting | bytes 32768
